TPU v7x, 128 devices: a whole 4x4x4 slice. The times are simulated.
128 devices in a mesh: cache: 16 (over x, z), cls: 8 (over y, core).
Axes of the slice: x: 4, y: 4, z: 4, core: 2. Of those that a mesh axis runs over, the one named last changes fastest.
Arguments:
- queries: bfloat16 [4096, 1024], P(('cache', 'cls')), may hold values from -14 to 14
- cache_keys: bfloat16 [163840, 1024], P('cache'), may hold values from -6 to 6
- labels: int32 [163840], P('cache'), may hold values from 0 to 10239, as said below
- prototypes: bfloat16 [10240, 1024], P('cls'), may hold values from -1 to 1
Outputs:
- log_probs: float32 [4096, 10240], P('cache', 'cls')
Inputs may be any that keep to these rules, and one draw needn't show every extreme that they name: Split the classes into 16 aligned blocks of 640; the 10240 cached shapes of one index of cache hold at most 1280 labels of one block, and one block, drawn from the seed, holds exactly 1280 labels of every index of cache.
All inputs are finite; a program needn't handle non-finite values.
Results may differ from a plain program's by a relative error of at most 0.0009.
The roundings to bfloat16 on the way count: a program that leaves them out, or rounds other values in their place, can miss the bound.
Values may be sent and summed in bfloat16 or wider, within the bound.
No kernel may reach another device: no remote copies, remote signals or barrier semaphores. Data moves between devices by JAX's collectives and lax.ppermute only.
A program may use at most 192 MiB of HBM per device.

v0:
```python
import jax
import jax.numpy as jnp
from jax import lax
from jax.sharding import PartitionSpec as P

text_scale = 100.0
epsilon = 1e-06


def combined_all(value, axis, join):
    pieces = jax.tree.map(lambda part: lax.all_gather(part, axis), value)
    head = jax.tree.map(lambda part: part[0], pieces)
    tail = jax.tree.map(lambda part: part[1:], pieces)
    total, _ = lax.scan(lambda total, share: (join(total, share), None), head, tail)
    return total


def unit_rows(matrix):
    widened = matrix.astype(jnp.float32)
    return (widened / jnp.sqrt(jnp.sum(widened * widened, axis=1, keepdims=True) + epsilon)).astype(
        jnp.bfloat16
    )


def affinity(unit_keys, shard_rows):
    sharpness = float(unit_keys.shape[1]) ** 0.5
    cosine = lax.dot_general(
        unit_keys, shard_rows, (((1,), (1,)), ((), ())), preferred_element_type=jnp.float32
    )
    return jnp.exp(sharpness * cosine).astype(jnp.bfloat16)


def combine(earlier, latter):
    highest = jnp.maximum(earlier[0], latter[0])
    return (
        highest,
        earlier[1] * jnp.exp(earlier[0] - highest) + latter[1] * jnp.exp(latter[0] - highest),
    )


def per_device(queries, cache_keys, labels, prototypes):
    unit_queries = unit_rows(queries)
    unit_keys = unit_rows(cache_keys)
    classes = prototypes.shape[0] * lax.axis_size("cls")
    scores = affinity(unit_keys, lax.all_gather(unit_queries, "cache", axis=0, tiled=True))
    scores = lax.optimization_barrier(scores).astype(jnp.float32)
    scored = jax.ops.segment_sum(scores, labels, num_segments=classes)
    totals = lax.psum_scatter(scored, "cache", scatter_dimension=1, tiled=True)
    columns = lax.all_to_all(totals, "cls", split_axis=0, concat_axis=1, tiled=True)
    text_logits = text_scale * lax.dot_general(
        lax.all_gather(unit_queries, "cls", axis=0, tiled=True),
        prototypes,
        (((1,), (1,)), ((), ())),
        preferred_element_type=jnp.float32,
    )
    logits = text_logits + columns.T
    local_max = jnp.max(logits, axis=1)
    local_total = jnp.sum(jnp.exp(logits - local_max[:, None]), axis=1)
    row_max, row_total = combined_all((local_max, local_total), "cls", combine)
    return logits - row_max[:, None] - jnp.log(row_total)[:, None]


def solution(mesh):
    placed = (P(("cache", "cls"), None), P("cache", None), P("cache"), P("cls", None))
    return jax.shard_map(
        per_device, mesh=mesh, in_specs=placed, out_specs=P("cache", "cls"), check_vma=False
    )
```

profile of v0, /device:TPU:1, one launch (start us, length us, event | category | flops | bytes accessed | tf_op | source)
XLA Modules:
  0.0 368.5 jit_solution(12241396914388293847)
XLA Ops:
  6.5 0.0 copy-start
  6.5 0.0 all-gather.6.cloned.1.call-start
  6.5 1.1 fusion.10
  7.7 1.6 fusion.11
  9.2 0.0 all-gather.6.cloned.1.call-update
  9.2 0.0 reduce-scatter.4.cloned.1.call-start
  9.3 8.8 %fusion = f32[10240]{0:T(1024)S(1)} fusion(bf16[10240,1024]{1,0:T(8,128)(2,1)} %param.7), kind=kLoop, calls=%fused_computation.6 | loop fusion | flops 31447040 | bytes 21012480 | tf_op jit(solution)/shard_map/reduce_sum | solution.py:20
  18.2 36.0 %all-gather.6.cloned.1.call-done = bf16[512,1024]{1,0:T(8,128)(2,1)} async-done(((bf16[32,1024]{1,0:T(8,128)(2,1)}), bf16[512,1024]{1,0:T(8,128)(2,1)}) %all-gather.6.cloned.1.call-update) | async-done | bytes 1048592 | tf_op jit(solution)/shard_map/all_gather | solution.py:45
  54.1 19.3 %exponential_convert_fusion = bf16[10240,512]{1,0:T(8,128)(2,1)} fusion(bf16[512,1024]{1,0:T(8,128)(2,1)} %all-gather.6.cloned.1.call-done, bf16[10240,1024]{1,0:T(8,128)(2,1)} %param.7, f32[10240]{0:T(1024)S(1)} %add_sqrt_fusion), kind=kOutput, calls=%fused_computation.10 | convolution fusion | flops 10779361280 | bytes 32546816 | tf_op jit(solution)/shard_map/dot_general | solution.py:27
  73.4 70.5 %scatter_custom_fusion = f32[10240,512]{1,0:T(8,128)} fusion(s32[10240]{0:T(1024)} %param.8, bf16[10240,512]{1,0:T(8,128)(2,1)} %exponential_convert_fusion, f32[]{:T(128)} %constant.12.clone.1), kind=kCustom, calls=%fused_computation.8 | custom fusion | flops 10485760 | bytes 31457792 | tf_op jit(solution)/shard_map/scatter-add | solution.py:47
  143.9 19.9 %copy.12 = f32[10240,512]{0,1:T(8,128)} copy(f32[10240,512]{1,0:T(8,128)} %scatter_custom_fusion) | data formatting | bytes 41943040
  163.8 0.0 reduce-scatter.4.cloned.1.call-update
  163.8 0.0 copy-start.2
  163.8 132.8 %reduce-scatter.4.cloned.1.call-done = f32[32,10240]{1,0:T(8,128)} async-done(((f32[512,10240]{1,0:T(8,128)}), f32[32,10240]{1,0:T(8,128)}) %reduce-scatter.4.cloned.1.call-update) | async-done | bytes 1310736
  296.6 4.6 %copy.13 = f32[10240,32]{1,0:T(8,128)} copy(f32[10240,32]{0,1:T(8,128)} %bitcast.29) | data formatting | bytes 2621440
  301.3 4.9 %copy.9 = f32[8,1280,32]{1,2,0:T(8,128)} copy(f32[8,1280,32]{2,1,0:T(8,128)} %bitcast.28) | data formatting | bytes 2621440 | tf_op jit(solution)/shard_map/all_to_all | solution.py:49
  306.1 4.9 %all-to-all-start = ((f32[8,1280,32]{1,2,0:T(8,128)}), f32[8,1280,32]{1,2,0:T(8,128)}, u32[]{:S(2)}, u32[]{:S(2)}) async-start(f32[8,1280,32]{1,2,0:T(8,128)} %copy.9), calls=%async_computation | async-start | bytes 2621440 | tf_op jit(solution)/shard_map/all_to_all | solution.py:49
  311.0 0.0 copy-done.2
  311.0 26.3 %all_gather.18 = bf16[256,1024]{1,0:T(8,128)(2,1)S(1)} all-gather(bf16[32,1024]{1,0:T(8,128)(2,1)S(1)} %copy-done.2), channel_id=1, replica_groups=mesh['cache'=16,'cls'=8] {'cls'}, dimensions={0}, use_global_device_ids=true | all-gather | bytes 589824 | tf_op jit(solution)/shard_map/all_gather | solution.py:51
  337.4 0.0 all-to-all-done
  337.4 0.0 copy-done
  337.4 2.3 fusion.12
  339.7 0.0 copy-start.1
  339.7 1.1 copy-done.1
  340.7 0.3 exponential_reduce_fusion
  341.1 8.7 %all-gather.3 = f32[8,1,256]{2,1,0:T(1,128)S(1)} all-gather(f32[1,1,256]{2,1,0:T(1,128)S(1)} %bitcast.37), channel_id=3, replica_groups=mesh['cache'=16,'cls'=8] {'cls'}, dimensions={0}, use_global_device_ids=true | all-gather | bytes 9216 | tf_op jit(solution)/shard_map/all_gather | solution.py:11
  349.8 8.9 %all-gather.2 = f32[8,1,256]{2,1,0:T(1,128)S(1)} all-gather(f32[1,1,256]{2,1,0:T(1,128)S(1)} %bitcast.36), channel_id=2, replica_groups=mesh['cache'=16,'cls'=8] {'cls'}, dimensions={0}, use_global_device_ids=true | all-gather | bytes 9216 | tf_op jit(solution)/shard_map/all_gather | solution.py:11
  358.7 0.3 while.12
  359.1 2.6 subtract_subtract_fusion
  (23 shorter events, 0.2 us)
Async XLA Ops:
  6.5 330.8 %copy-start = (bf16[1280,1024]{1,0:T(8,128)(2,1)S(1)}, bf16[1280,1024]{1,0:T(8,128)(2,1)}, u32[]{:S(2)}) copy-start(bf16[1280,1024]{1,0:T(8,128)(2,1)} %param.9) | copy-start | bytes 7864324
  6.5 47.6 %all-gather.6.cloned.1.call-start = ((), (), s32[]{:S(2)}) async-start(), calls=%async_computation.2 | async-start | bytes 1114112 | tf_op jit(solution)/shard_map/all_gather | solution.py:45
  9.2 287.4 %reduce-scatter.4.cloned.1.call-start = ((), (), s32[]{:S(2)}) async-start(), calls=%async_computation.3 | async-start | bytes 22282240
  163.8 147.2 %copy-start.2 = (bf16[32,1024]{1,0:T(8,128)(2,1)S(1)}, bf16[32,1024]{1,0:T(8,128)(2,1)}, u32[]{:S(2)}) copy-start(bf16[32,1024]{1,0:T(8,128)(2,1)} %fusion.11) | copy-start | bytes 196612
  306.1 31.2 %all-to-all-start = ((f32[8,1280,32]{1,2,0:T(8,128)}), f32[8,1280,32]{1,2,0:T(8,128)}, u32[]{:S(2)}, u32[]{:S(2)}) async-start(f32[8,1280,32]{1,2,0:T(8,128)} %copy.9), calls=%async_computation | async-start | bytes 2621440 | tf_op jit(solution)/shard_map/all_to_all | solution.py:49
  339.7 1.1 copy-start.1
Sparse Core Ops, SparseCore 0:
  9.5 44.5 all-gather.5
  163.9 132.6 reduce-scatter.3
where the time goes:
time: 369 us; the launch traced here: 368 us
  waiting for transfers between devices  169 us (46%)
  other arithmetic  85.1 us (23%)
  blocking collectives  43.9 us (12%)
  local copies, waits for them, and re-layouts  30.5 us (8%)
  matrix products  21.6 us (6%)
  between operations  13.5 us (4%)
  starting transfers between devices  4.95 us (1%)
    unnamed x3, waiting for transfers between devices  133 us
    scatter-add x1, other arithmetic, per_device(): scored = jax.ops.segment_sum(scores, labels, num_segments=classes)  70.5 us
    all_gather x1, waiting for transfers between devices, per_device(): lax.all_gather(unit_queries, 'cache', axis=0, tiled=True)  36 us
    all_gather x1, blocking collectives, per_device(): lax.all_gather(unit_queries, 'cls', axis=0, tiled=True)  26.3 us
    unnamed x10, local copies, waits for them, and re-layouts  25.6 us
    dot_general x1, matrix products, affinity(): lax.dot_general(unit_keys, shard_rows, (((1,), (1,)), ((), ())), preferre...  19.3 us
    all_gather x2, blocking collectives, combined_all(): pieces = jax.tree.map(lambda part: lax.all_gather(part, axis), value)  17.6 us
    reduce_sum x2, other arithmetic, unit_rows(): jnp.sum(widened * widened, axis=1, keepdims=True) + epsilon  9.95 us
  transfers between devices with their start and end apart: 3, of which 2 were waited for; matrix products, arithmetic and copies ran while one was open for 2% of the time, Pallas kernels for 0%

commit v1 on v0

v1 whole, which is shorter than its diff:
```python
import functools

import jax
import jax.numpy as jnp
from jax import lax
from jax.experimental import pallas as pl
from jax.experimental.pallas import tpu as pltpu
from jax.sharding import PartitionSpec as P

text_scale = 100.0
epsilon = 1e-06
SIDE = 4
CB = 640
CAP = 1280
QT = 256
KT = 256
TAIL = 16
VMEM_LIMIT = 40 * 1024 * 1024


def params():
    return pltpu.CompilerParams(vmem_limit_bytes=VMEM_LIMIT)


def unit_rows(matrix):
    widened = matrix.astype(jnp.float32)
    return (widened / jnp.sqrt(jnp.sum(widened * widened, axis=1, keepdims=True) + epsilon)).astype(
        jnp.bfloat16
    )


def prepare_kernel(rows_ref, labels_ref, unit_ref, hot_ref):
    unit_ref[...] = unit_rows(rows_ref[...])
    classes = lax.broadcasted_iota(jnp.int32, (KT, CB), 1)
    hot_ref[...] = jnp.where(labels_ref[...] == classes, 1.0, 0.0).astype(jnp.bfloat16)


def prepare(rows, labels):
    count, width = rows.shape
    return pl.pallas_call(
        prepare_kernel,
        grid=(count // KT,),
        in_specs=[
            pl.BlockSpec((KT, width), lambda i: (i, 0)),
            pl.BlockSpec((KT, 1), lambda i: (i, 0)),
        ],
        out_specs=[
            pl.BlockSpec((KT, width), lambda i: (i, 0)),
            pl.BlockSpec((KT, CB), lambda i: (i, 0)),
        ],
        out_shape=[
            jax.ShapeDtypeStruct((count, width), jnp.bfloat16),
            jax.ShapeDtypeStruct((count, CB), jnp.bfloat16),
        ],
        compiler_params=params(),
        cost_estimate=pl.CostEstimate(flops=count * width * 4, bytes_accessed=count * width * 6, transcendentals=count),
        name="prepare",
    )(rows, labels)


def diagonal():
    shape = (QT, QT)
    return lax.broadcasted_iota(jnp.int32, shape, 0) == lax.broadcasted_iota(jnp.int32, shape, 1)


def encode(values, message_ref, tile, tail_row):
    largest = jnp.maximum(jnp.max(values, axis=1, keepdims=True), 1e-30)
    exponent = jnp.ceil(jnp.log2(largest) - 14.99)
    codes = (values * jnp.exp2(-exponent) + 0.5).astype(jnp.int32)
    message_ref[pl.ds(tile * QT, QT), :] = codes.astype(jnp.int16)
    along = jnp.sum(jnp.where(diagonal(), exponent, 0.0), axis=0, keepdims=True)
    shape = (TAIL, QT)
    old = message_ref[tail_row : tail_row + TAIL, :QT].astype(jnp.int32)
    new = jnp.broadcast_to(along, shape).astype(jnp.int32)
    at = lax.broadcasted_iota(jnp.int32, shape, 0) == tile
    message_ref[tail_row : tail_row + TAIL, :QT] = jnp.where(at, new, old).astype(jnp.int16)


def clear_tail(message_ref, tail_row):
    message_ref[tail_row : tail_row + TAIL, :] = jnp.zeros((TAIL, CB), jnp.int16)


def decode(message_ref, tile, tail_row):
    shape = (TAIL, QT)
    tail = message_ref[tail_row : tail_row + TAIL, :QT].astype(jnp.float32)
    at = lax.broadcasted_iota(jnp.int32, shape, 0) == tile
    along = jnp.sum(jnp.where(at, tail, 0.0), axis=0, keepdims=True)
    exponent = jnp.sum(jnp.where(diagonal(), along, 0.0), axis=1, keepdims=True)
    codes = message_ref[pl.ds(tile * QT, QT), :].astype(jnp.float32)
    return codes * jnp.exp2(exponent)


HALF = 2 * QT
HALF_MSG = jax.ShapeDtypeStruct((HALF + TAIL, CB), jnp.int16)
TILE_MSG = jax.ShapeDtypeStruct((QT + TAIL, CB), jnp.int16)


def tile_sums(tiles, q_ref, keys_ref, hot_ref, total_ref):
    sharpness = float(q_ref.shape[-1]) ** 0.5
    total_ref[...] = jnp.zeros_like(total_ref)

    def step(t, carry):
        at = pl.ds(t * KT, KT)
        cosine = lax.dot_general(
            q_ref[0], keys_ref[at, :], (((1,), (1,)), ((), ())), preferred_element_type=jnp.float32
        )
        scores = jnp.exp(sharpness * cosine).astype(jnp.bfloat16)
        total_ref[...] += jnp.dot(scores, hot_ref[at, :], preferred_element_type=jnp.float32)
        return carry

    lax.fori_loop(0, tiles, step, 0)


def sums(targets, messages, raws, plan, queries, keys, hots):
    steps, width = len(targets), keys.shape[1]
    out_shape = [HALF_MSG] * messages
    out_specs = [pl.BlockSpec(HALF_MSG.shape, lambda i, p: (0, 0))] * messages
    if raws:
        out_shape.append(jax.ShapeDtypeStruct((raws, QT, CB), jnp.float32))
        out_specs.append(pl.BlockSpec((raws, QT, CB), lambda i, p: (0, 0, 0)))

    def kernel(plan_ref, q_ref, keys_ref, hot_ref, *rest):
        outs, total_ref = rest[:-1], rest[-1]
        step = pl.program_id(0)
        tile_sums(plan_ref[2, step], q_ref, keys_ref, hot_ref, total_ref)
        for index, (out, tile) in enumerate(targets):
            @pl.when(step == index)
            def _(out=out, tile=tile):
                if out < 0:
                    outs[-1][tile] = total_ref[...]
                else:
                    if tile == 0:
                        clear_tail(outs[out], HALF)
                    encode(total_ref[...], outs[out], tile, HALF)

    return pl.pallas_call(
        kernel,
        grid_spec=pltpu.PrefetchScalarGridSpec(
            num_scalar_prefetch=1,
            grid=(steps,),
            in_specs=[
                pl.BlockSpec((1, QT, width), lambda i, p: (p[0, i], 0, 0)),
                pl.BlockSpec((CAP, width), lambda i, p: (p[1, i], 0)),
                pl.BlockSpec((CAP, CB), lambda i, p: (p[1, i], 0)),
            ],
            out_specs=out_specs,
            scratch_shapes=[pltpu.VMEM((QT, CB), jnp.float32)],
        ),
        out_shape=out_shape,
        compiler_params=params(),
        cost_estimate=pl.CostEstimate(
            flops=steps * 2 * QT * CAP * (width + CB),
            bytes_accessed=2 * CAP * (width + CB) * 2,
            transcendentals=steps * QT * CAP,
        ),
        name="sums",
    )(plan, queries, keys, hots)


def forward(raw, arrived):
    count = len(arrived)

    def kernel(raw_ref, *rest):
        for m in range(count):
            source, target = rest[m], rest[count + m]
            clear_tail(target, HALF)

            def body(t, carry, m=m, source=source, target=target):
                encode(raw_ref[2 * m + t] + decode(source, t, HALF), target, t, HALF)
                return carry

            lax.fori_loop(0, 2, body, 0)

    return pl.pallas_call(
        kernel,
        out_shape=[HALF_MSG] * count,
        compiler_params=params(),
        cost_estimate=pl.CostEstimate(flops=10 * count * HALF * CB, bytes_accessed=8 * count * HALF * CB, transcendentals=0),
        name="forward",
    )(raw, *arrived)


def turn(place, raw, first_a, first_b, second_a, second_b):
    def kernel(place_ref, raw_ref, fa, fb, sa, sb, own_ref, plus_ref, far_ref, minus_ref, total_ref):
        for k, out in enumerate((None, plus_ref, far_ref, minus_ref)):
            tile = lax.rem(place_ref[0] + k, SIDE)

            @pl.when(tile < 2)
            def _():
                total_ref[...] = raw_ref[tile] + decode(fa, tile, HALF) + decode(fb, tile, HALF)

            @pl.when(tile >= 2)
            def _():
                total_ref[...] = raw_ref[tile] + decode(sa, tile - 2, HALF) + decode(sb, tile - 2, HALF)

            if out is None:
                own_ref[...] = total_ref[...]
            else:
                clear_tail(out, QT)
                encode(total_ref[...], out, 0, QT)

    vmem = pl.BlockSpec(memory_space=pltpu.VMEM)
    return pl.pallas_call(
        kernel,
        in_specs=[pl.BlockSpec(memory_space=pltpu.SMEM)] + [vmem] * 5,
        out_specs=[vmem] * 4,
        out_shape=[jax.ShapeDtypeStruct((QT, CB), jnp.float32), TILE_MSG, TILE_MSG, TILE_MSG],
        scratch_shapes=[pltpu.VMEM((QT, CB), jnp.float32)],
        compiler_params=params(),
        cost_estimate=pl.CostEstimate(flops=40 * QT * CB, bytes_accessed=40 * QT * CB, transcendentals=0),
        name="turn",
    )(place, raw, first_a, first_b, second_a, second_b)


def close(text, own_a, msgs_a, own_b, msgs_b):
    def kernel(text_ref, *rest):
        own, msgs = rest[0:2], (rest[2:5], rest[5:8])
        logits_ref, stats_ref = rest[8:]
        for block in range(2):
            total = own[block][...]
            for msg in msgs[block]:
                total += decode(msg, 0, QT)
            at = slice(block * CB, block * CB + CB)
            logits_ref[:, at] = text_ref[:, at] + total
        logits = logits_ref[...]
        largest = jnp.max(logits, axis=1, keepdims=True)
        total = jnp.sum(jnp.exp(logits - largest), axis=1, keepdims=True)
        eye = diagonal()
        stats_ref[0:1, :] = jnp.sum(jnp.where(eye, largest, 0.0), axis=0, keepdims=True)
        stats_ref[1:2, :] = jnp.sum(jnp.where(eye, total, 0.0), axis=0, keepdims=True)

    return pl.pallas_call(
        kernel,
        out_shape=[
            jax.ShapeDtypeStruct((QT, 2 * CB), jnp.float32),
            jax.ShapeDtypeStruct((2, QT), jnp.float32),
        ],
        compiler_params=params(),
        cost_estimate=pl.CostEstimate(flops=30 * QT * CB, bytes_accessed=40 * QT * CB, transcendentals=QT * CB),
        name="close",
    )(text, own_a, own_b, *msgs_a, *msgs_b)


def finish(logits, stats):
    def kernel(logits_ref, stats_ref, out_ref):
        largest = jnp.max(stats_ref[:, 0, :], axis=0, keepdims=True)
        total = jnp.sum(stats_ref[:, 1, :] * jnp.exp(stats_ref[:, 0, :] - largest), axis=0, keepdims=True)
        eye = diagonal()
        largest = jnp.sum(jnp.where(eye, largest, 0.0), axis=1, keepdims=True)
        shift = jnp.sum(jnp.where(eye, jnp.log(total), 0.0), axis=1, keepdims=True)
        out_ref[...] = logits_ref[...] - largest - shift

    return pl.pallas_call(
        kernel,
        out_shape=jax.ShapeDtypeStruct(logits.shape, jnp.float32),
        compiler_params=params(),
        name="finish",
    )(logits, stats)


def shifted(dx, dz):
    return [
        (x * SIDE + z, (x + dx) % SIDE * SIDE + (z + dz) % SIDE) for x in range(SIDE) for z in range(SIDE)
    ]


def send(message, dx, dz):
    return lax.ppermute(message, "cache", shifted(dx, dz))


def per_device(queries, cache_keys, labels, prototypes):
    width = queries.shape[1]
    own = lax.axis_index("cache")
    x, z = own // SIDE, own % SIDE
    low = lax.axis_index("cls") * (2 * CB)

    unit_queries = lax.all_gather(unit_rows(queries), ("cache", "cls"), axis=0, tiled=True)

    order = lax.sort(labels * 16384 + lax.iota(jnp.int32, labels.shape[0]), is_stable=False)
    start = jnp.sum((labels < low).astype(jnp.int32))
    middle = jnp.sum((labels < low + CB).astype(jnp.int32))
    stop = jnp.sum((labels < low + 2 * CB).astype(jnp.int32))
    padded = jnp.concatenate([order, jnp.zeros((CAP,), jnp.int32)])
    picked = jnp.concatenate(
        [lax.dynamic_slice(padded, (start,), (CAP,)), lax.dynamic_slice(padded, (middle,), (CAP,))]
    )
    counts = jnp.stack([middle - start, stop - middle])
    place = lax.iota(jnp.int32, 2 * CAP)
    block = place // CAP
    valid = place - block * CAP < jnp.where(block == 0, counts[0], counts[1])
    local = jnp.where(valid, picked // 16384 - low - block * CB, -1)
    rows = jnp.take(cache_keys, picked % 16384, axis=0, mode="clip")
    keys, hots = prepare(rows, local[:, None])
    tiles = (counts + KT - 1) // KT

    q3 = unit_queries.reshape(SIDE * SIDE, QT, width)
    text = text_scale * lax.dot_general(
        lax.dynamic_index_in_dim(q3, own, 0, keepdims=False),
        prototypes,
        (((1,), (1,)), ((), ())),
        preferred_element_type=jnp.float32,
    )

    def steps_a(dx, parts):
        return [(0, (x + dx) % SIDE * SIDE + j) for j in parts]

    def steps_b(dz, parts):
        return [(1, j * SIDE + (z + dz) % SIDE) for j in parts]

    def plan(steps):
        chunks = jnp.stack([chunk for _, chunk in steps])
        blocks = jnp.array([b for b, _ in steps], jnp.int32)
        return jnp.stack([chunks.astype(jnp.int32), blocks, jnp.stack([tiles[b] for b, _ in steps])])

    run = functools.partial(sums, queries=q3, keys=keys, hots=hots)
    low_half, high_half, all_four = (0, 1), (2, 3), (0, 1, 2, 3)

    pa_right, pa_left, pb_right, pb_left = run(
        [(m, t) for m in range(4) for t in range(2)],
        4,
        0,
        plan(steps_a(2, all_four) + steps_b(2, all_four)),
    )
    pa_right, pa_left = send(pa_right, 1, 0), send(pa_left, -1, 0)
    pb_right, pb_left = send(pb_right, 0, 1), send(pb_left, 0, -1)

    qa_right, qa_left, qb_right, qb_left = run(
        [(m, t) for m in range(4) for t in range(2)],
        4,
        0,
        plan(steps_a(1, high_half) + steps_a(3, low_half) + steps_b(1, high_half) + steps_b(3, low_half)),
    )
    qa_right, qa_left = send(qa_right, 1, 0), send(qa_left, -1, 0)
    qb_right, qb_left = send(qb_right, 0, 1), send(qb_left, 0, -1)
    (raw,) = run(
        [(-1, t) for t in range(8)],
        0,
        8,
        plan(steps_a(1, low_half) + steps_a(3, high_half) + steps_b(1, low_half) + steps_b(3, high_half)),
    )
    ra_right, ra_left, rb_right, rb_left = forward(raw, (pa_right, pa_left, pb_right, pb_left))
    ra_right, ra_left = send(ra_right, 1, 0), send(ra_left, -1, 0)
    rb_right, rb_left = send(rb_right, 0, 1), send(rb_left, 0, -1)
    (mine,) = run([(-1, t) for t in range(8)], 0, 8, plan(steps_a(0, all_four) + steps_b(0, all_four)))

    own_a, a_plus, a_far, a_minus = turn(z[None], mine[:4], ra_right, qa_left, qa_right, ra_left)
    own_b, b_plus, b_far, b_minus = turn(x[None], mine[4:], rb_right, qb_left, qb_right, rb_left)
    a_msgs = send(a_plus, 0, 1), send(a_far, 0, 2), send(a_minus, 0, -1)
    b_msgs = send(b_plus, 1, 0), send(b_far, 2, 0), send(b_minus, -1, 0)

    logits, stats = close(text, own_a, a_msgs, own_b, b_msgs)
    return finish(logits, lax.all_gather(stats, "cls"))


def solution(mesh):
    placed = (P(("cache", "cls"), None), P("cache", None), P("cache"), P("cls", None))
    return jax.shard_map(
        per_device, mesh=mesh, in_specs=placed, out_specs=P("cache", "cls"), check_vma=False
    )
```

time: 369 us -> 283 us (0.77)
  the two profiles are of different devices: /device:TPU:1 before, /device:TPU:5 now
where the time goes in v1:
time: 283 us; the launch traced here: 281 us
  Pallas kernels  105 us (37%)
  waiting for transfers between devices  59.1 us (21%)
  local copies, waits for them, and re-layouts  41.8 us (15%)
  starting transfers between devices  27 us (10%)
  between operations  20.1 us (7%)
  other arithmetic  15.1 us (5%)
  blocking collectives  10.9 us (4%)
    pallas_call x4, Pallas kernels, sums(): pl.pallas_call(kernel, grid_spec=pltpu.PrefetchScalarGridSpec(num_scalar_...  85.3 us
    ppermute x18, waiting for transfers between devices, send(): return lax.ppermute(message, 'cache', shifted(dx, dz))  46.1 us
    ppermute x18, starting transfers between devices, send(): return lax.ppermute(message, 'cache', shifted(dx, dz))  27 us
    gather x1, local copies, waits for them, and re-layouts, per_device(): rows = jnp.take(cache_keys, picked % 16384, axis=0, mode='clip')  21.8 us
    unnamed x24, local copies, waits for them, and re-layouts  13.3 us
    all_gather x1, waiting for transfers between devices, per_device(): lax.all_gather(unit_rows(queries), ('cache', 'cls'), axis=0, tiled=True)  13 us
    all_gather x1, blocking collectives, per_device(): return finish(logits, lax.all_gather(stats, 'cls'))  10.9 us
    pallas_call x1, Pallas kernels, prepare(): pl.pallas_call(prepare_kernel, grid=(count // KT,), in_specs=[pl.BlockSpe...  7.26 us
  transfers between devices with their start and end apart: 19, of which 7 were waited for; matrix products, arithmetic and copies ran while one was open for 15% of the time, Pallas kernels for 28%

profile of v1, /device:TPU:5, one launch (start us, length us, event | category | flops | bytes accessed | tf_op | source)
XLA Modules:
  0.0 281.4 jit_solution(4573482944122942897)
XLA Ops:
  6.5 1.1 fusion.12
  7.7 1.6 fusion.13
  9.2 0.0 all-gather.4.cloned.1.call-update
  9.3 1.5 convert_reduce_fusion.1
  14.7 6.3 %sort.7 = s32[10240]{0:T(1024)S(1)} sort(s32[10240]{0:T(1024)S(1)} %get-tuple-element.62), dimensions={0}, to_apply=%region_4.5 | sort | flops 143360 | bytes 81920 | tf_op jit(solution)/shard_map/sort | solution.py:279
  22.3 0.1 pad_dynamic-slice_fusion.1
  22.4 1.5 copy.11
  25.2 4.5 %fusion.3 = (s32[2560,1]{1,0:T(8,128)}, s32[2560]{0:T(1024)S(1)}) fusion(s32[2560,1]{1,0:T(8,128)} %copy.11, s32[]{:T(128)S(6)} %mul.70, s32[]{:T(128)} %sub.68, s32[]{:T(128)} %sub.67), kind=kLoop, calls=%fused_computation.15 | loop fusion | flops 92160 | bytes 30732 | tf_op jit(solution)/shard_map/jit(_where)/select_n | solution.py:291
  29.7 21.8 %gather_fusion = bf16[2560,1024]{1,0:T(8,128)(2,1)} fusion(bf16[10240,1024]{1,0:T(8,128)(2,1)} %param.9, s32[3072]{0:T(1024)S(1)} %pad_clamp_fusion), kind=kCustom, calls=%fused_computation | custom fusion | bytes 10496000 | tf_op jit(solution)/shard_map/jit(_take)/gather | solution.py:292
  51.5 0.1 and_select_fusion
  51.6 0.6 fusion.16
  52.2 3.8 %stack.180 = s32[8]{0:T(128)S(1)} concatenate(s32[1]{0:T(128)} %get-tuple-element.68, s32[1]{0:T(128)} %get-tuple-element.68, s32[1]{0:T(128)} %get-tuple-element.68, s32[2]{0:T(128)S(1)} %and_select_fusion, s32[1]{0:T(128)} %get-tuple-element.67, s32[1]{0:T(128)} %get-tuple-element.67, s32[1]{0:T(128)} %get-tuple-element.67), dimensions={0} | concatenate | bytes 64 | tf_op jit(solution)/shard_map/stack | solution.py:313
  56.0 0.1 stack.174
  56.1 0.1 stack.203
  56.1 0.1 stack.191
  56.2 0.1 stack.215
  56.3 1.3 copy-done.1
  57.7 7.3 %prepare.1 = (bf16[2560,1024]{1,0:T(8,128)(2,1)S(1)}, bf16[2560,640]{1,0:T(8,128)(2,1)S(1)}) custom-call(bf16[2560,1024]{1,0:T(8,128)(2,1)} %gather_fusion, s32[2560,1]{1,0:T(8,128)S(1)} %copy-done.1), custom_call_target="tpu_custom_call" | custom-call | flops 10485760 | bytes 15728640 | tf_op jit(solution)/shard_map/prepare/pallas_call | solution.py:40
  64.9 2.4 copy-done.6
  67.3 1.7 copy-done.8
  69.0 13.0 %all-gather.4.cloned.1.call-done = bf16[4096,1024]{1,0:T(8,128)(2,1)} async-done(((bf16[32,1024]{1,0:T(8,128)(2,1)}), bf16[4096,1024]{1,0:T(8,128)(2,1)}) %all-gather.4.cloned.1.call-update) | async-done | bytes 8388624 | tf_op jit(solution)/shard_map/all_gather | solution.py:277
  82.0 2.5 copy-done.7
  84.5 1.9 copy-done.9
  86.4 22.7 %sums.6 = (s16[528,640]{1,0:T(8,128)(2,1)S(1)}, s16[528,640]{1,0:T(8,128)(2,1)S(1)}, s16[528,640]{1,0:T(8,128)(2,1)}, s16[528,640]{1,0:T(8,128)(2,1)}) custom-call(s32[3,8]{1,0:T(4,128)S(1)} %get-tuple-element.65.plan_ref, bf16[16,256,1024]{2,1,0:T(8,128)(2,1)} %bitcast.48, bf16[2560,1024]{1,0:T(8,128)(2,1)S(1)} %copy-done.7, bf16[2560,640]{1,0:T(8,128)(2,1)S(1)} %copy-done.9), custom_call_target="tpu_custom_call" | custom-call | flops 8724152320 | bytes 8519680 | tf_op jit(solution)/shard_map/sums/pallas_call | solution.py:136
  109.2 0.0 collective-permute-start
  109.2 1.5 collective-permute-start.1
  110.6 6.4 %collective-permute-start.2 = (s16[528,640]{1,0:T(8,128)(2,1)}, s16[528,640]{1,0:T(8,128)(2,1)S(1)}, u32[]{:S(2)}, u32[]{:S(2)}) collective-permute-start(s16[528,640]{1,0:T(8,128)(2,1)} %get-tuple-element.33), channel_id=1, source_target_pairs={{0,8},{8,16},{16,24},{24,0},{32,40},{40,48},{48,56},{56,32},{64,72... | collective-permute-start | bytes 2027528 | tf_op jit(solution)/shard_map/ppermute | solution.py:268
  117.1 0.0 collective-permute-start.3
  117.1 22.4 %sums.7 = (s16[528,640]{1,0:T(8,128)(2,1)S(1)}, s16[528,640]{1,0:T(8,128)(2,1)S(1)}, s16[528,640]{1,0:T(8,128)(2,1)}, s16[528,640]{1,0:T(8,128)(2,1)S(1)}) custom-call(s32[3,8]{1,0:T(4,128)S(1)} %get-tuple-element.63.plan_ref, bf16[16,256,1024]{2,1,0:T(8,128)(2,1)} %bitcast.49, bf16[2560,1024]{1,0:T(8,128)(2,1)S(1)} %copy-done.7, bf16[2560,640]{1,0:T(8,128)(2,1)S(1)} %copy-done.9), custom_call_target="tpu_custom_call" | custom-call | flops 8724152320 | bytes 8519680 | tf_op jit(solution)/shard_map/sums/pallas_call | solution.py:136
  139.5 7.3 %collective-permute-start.10 = (s16[528,640]{1,0:T(8,128)(2,1)}, s16[528,640]{1,0:T(8,128)(2,1)S(1)}, u32[]{:S(2)}, u32[]{:S(2)}) collective-permute-start(s16[528,640]{1,0:T(8,128)(2,1)} %get-tuple-element.42), channel_id=1, source_target_pairs={{0,8},{8,16},{16,24},{24,0},{32,40},{40,48},{48,56},{56,32},{64,72... | collective-permute-start | bytes 2027528 | tf_op jit(solution)/shard_map/ppermute | solution.py:268
  146.8 20.1 %sums.5.raw_ref = f32[8,256,640]{2,1,0:T(8,128)S(1)} custom-call(s32[3,8]{1,0:T(4,128)S(1)} %get-tuple-element.64.plan_ref, bf16[16,256,1024]{2,1,0:T(8,128)(2,1)} %bitcast.50, bf16[2560,1024]{1,0:T(8,128)(2,1)S(1)} %copy-done.7, bf16[2560,640]{1,0:T(8,128)(2,1)S(1)} %copy-done.9), custom_call_target="tpu_custom_call" | custom-call | flops 8724152320 | bytes 8519680 | tf_op jit(solution)/shard_map/sums/pallas_call | solution.py:136
  166.9 0.1 collective-permute-start.9
  167.0 0.0 collective-permute-done.2.rest_2_
  167.0 0.0 collective-permute-done.3.rest_3_
  167.0 3.9 %forward.1 = (s16[528,640]{1,0:T(8,128)(2,1)}, s16[528,640]{1,0:T(8,128)(2,1)}, s16[528,640]{1,0:T(8,128)(2,1)}, s16[528,640]{1,0:T(8,128)(2,1)}) custom-call(f32[8,256,640]{2,1,0:T(8,128)S(1)} %sums.5.raw_ref, s16[528,640]{1,0:T(8,128)(2,1)S(1)} %collective-permute-done.rest_0_, s16[528,640]{1,0:T(8,128)(2,1)S(1)} %collective-permute-done.1.rest_1_, ...), custom_call_target="tpu_custom_call" | custom-call | flops 13107200 | bytes 10485760 | tf_op jit(solution)/shard_map/forward/pallas_call | solution.py:174
  170.9 5.8 %collective-permute-start.8 = (s16[528,640]{1,0:T(8,128)(2,1)}, s16[528,640]{1,0:T(8,128)(2,1)S(1)}, u32[]{:S(2)}, u32[]{:S(2)}) collective-permute-start(s16[528,640]{1,0:T(8,128)(2,1)} %get-tuple-element.40), channel_id=1, source_target_pairs={{0,8},{8,16},{16,24},{24,0},{32,40},{40,48},{48,56},{56,32},{64,72... | collective-permute-start | bytes 2027528 | tf_op jit(solution)/shard_map/ppermute | solution.py:268
  176.7 1.9 copy-done.10
  178.6 20.1 %sums.4 = f32[8,256,640]{2,1,0:T(8,128)S(1)} custom-call(s32[3,8]{1,0:T(4,128)S(1)} %get-tuple-element.66.plan_ref, bf16[16,256,1024]{2,1,0:T(8,128)(2,1)} %bitcast.51, bf16[2560,1024]{1,0:T(8,128)(2,1)S(1)} %copy-done.7, bf16[2560,640]{1,0:T(8,128)(2,1)S(1)} %copy-done.10), custom_call_target="tpu_custom_call" | custom-call | flops 8724152320 | bytes 8519680 | tf_op jit(solution)/shard_map/sums/pallas_call | solution.py:136
  198.7 0.1 collective-permute-start.5
  198.8 0.0 collective-permute-done.10.sa
  198.8 1.4 collective-permute-start.6
  200.2 0.0 collective-permute-done.9.fb
  200.3 0.1 collective-permute-start.4
  200.3 1.4 collective-permute-start.7
  201.7 0.3 fusion.15
  202.1 2.8 turn.3
  204.9 0.1 collective-permute-start.15
  205.0 9.4 %collective-permute-done.5.fb = s16[528,640]{1,0:T(8,128)(2,1)S(1)} collective-permute-done((s16[528,640]{1,0:T(8,128)(2,1)S(1)}, s16[528,640]{1,0:T(8,128)(2,1)S(1)}, u32[]{:S(2)}, u32[]{:S(2)}) %collective-permute-start.5) | collective-permute-done | bytes 675872 | tf_op jit(solution)/shard_map/ppermute | solution.py:268
  214.3 1.8 collective-permute-done.6.sa
  216.1 1.0 collective-permute-start.17
  217.2 20.9 %collective-permute-done.4.fa = s16[528,640]{1,0:T(8,128)(2,1)S(1)} collective-permute-done((s16[528,640]{1,0:T(8,128)(2,1)}, s16[528,640]{1,0:T(8,128)(2,1)S(1)}, u32[]{:S(2)}, u32[]{:S(2)}) %collective-permute-start.4) | collective-permute-done | bytes 675872 | tf_op jit(solution)/shard_map/ppermute | solution.py:268
  238.1 2.5 turn.2
  240.6 0.8 copy-done.2
  241.4 0.0 collective-permute-start.12
  241.4 0.8 collective-permute-done.15.rest_5_
  242.3 0.8 copy-done.4
  243.0 1.8 collective-permute-start.14
  244.9 2.0 convolution_multiply_fusion.text_ref
  246.9 0.0 collective-permute-done.17.rest_7_
  246.9 12.2 %collective-permute-done.12.rest_2_ = s16[272,640]{1,0:T(8,128)(2,1)} collective-permute-done((s16[272,640]{1,0:T(8,128)(2,1)}, s16[272,640]{1,0:T(8,128)(2,1)}, u32[]{:S(2)}, u32[]{:S(2)}) %collective-permute-start.12) | collective-permute-done | bytes 348192 | tf_op jit(solution)/shard_map/ppermute | solution.py:268
  259.1 0.9 collective-permute-done.14.rest_4_
  260.0 2.4 close.1
  262.4 10.9 %all-gather.1.stats_ref = f32[8,2,256]{2,1,0:T(2,128)S(1)} all-gather(f32[1,2,256]{2,1,0:T(2,128)S(1)} %bitcast.47), channel_id=2, replica_groups=mesh['cache'=16,'cls'=8] {'cls'}, dimensions={0}, use_global_device_ids=true | all-gather | bytes 18432 | tf_op jit(solution)/shard_map/all_gather | solution.py:352
  273.3 1.3 finish.1
  (33 shorter events, 0.1 us)
Async XLA Ops:
  6.5 238.3 %copy-start = (bf16[1280,1024]{1,0:T(8,128)(2,1)S(1)}, bf16[1280,1024]{1,0:T(8,128)(2,1)}, u32[]{:S(2)}) copy-start(bf16[1280,1024]{1,0:T(8,128)(2,1)} %param.11) | copy-start | bytes 7864324
  6.5 75.5 %all-gather.4.cloned.1.call-start = ((), (), s32[]{:S(2)}) async-start(), calls=%async_computation | async-start | bytes 8454144 | tf_op jit(solution)/shard_map/all_gather | solution.py:277
  56.3 1.3 copy-start.1
  57.7 11.3 %copy-start.11 = (s32[1,8]{1,0:T(1,128)S(1)}, s32[1,8]{1,0:T(1,128)}, u32[]{:S(2)}) copy-start(s32[1,8]{1,0:T(1,128)} %constant.197) | copy-start | bytes 100
  64.9 2.4 copy-start.6
  67.3 1.7 copy-start.8
  82.0 2.5 copy-start.7
  84.5 1.9 copy-start.9
  109.2 57.7 %collective-permute-start = (s16[528,640]{1,0:T(8,128)(2,1)S(1)}, s16[528,640]{1,0:T(8,128)(2,1)S(1)}, u32[]{:S(2)}, u32[]{:S(2)}) collective-permute-start(s16[528,640]{1,0:T(8,128)(2,1)S(1)} %get-tuple-element.31), channel_id=1, source_target_pairs={{0,32},{8,40},{16,48},{24,56},{32,64},{40,72},{48,80},{56,88},{64,... | collective-permute-start | bytes 2027528 | tf_op jit(solution)/shard_map/ppermute | solution.py:268
  109.2 57.8 %collective-permute-start.1 = (s16[528,640]{1,0:T(8,128)(2,1)S(1)}, s16[528,640]{1,0:T(8,128)(2,1)S(1)}, u32[]{:S(2)}, u32[]{:S(2)}) collective-permute-start(s16[528,640]{1,0:T(8,128)(2,1)S(1)} %get-tuple-element.32), channel_id=1, source_target_pairs={{0,96},{8,104},{16,112},{24,120},{32,0},{40,8},{48,16},{56,24},{64... | collective-permute-start | bytes 2027528 | tf_op jit(solution)/shard_map/ppermute | solution.py:268
  110.6 56.3 %collective-permute-start.2 = (s16[528,640]{1,0:T(8,128)(2,1)}, s16[528,640]{1,0:T(8,128)(2,1)S(1)}, u32[]{:S(2)}, u32[]{:S(2)}) collective-permute-start(s16[528,640]{1,0:T(8,128)(2,1)} %get-tuple-element.33), channel_id=1, source_target_pairs={{0,8},{8,16},{16,24},{24,0},{32,40},{40,48},{48,56},{56,32},{64,72... | collective-permute-start | bytes 2027528 | tf_op jit(solution)/shard_map/ppermute | solution.py:268
  117.1 49.9 %collective-permute-start.3 = (s16[528,640]{1,0:T(8,128)(2,1)}, s16[528,640]{1,0:T(8,128)(2,1)S(1)}, u32[]{:S(2)}, u32[]{:S(2)}) collective-permute-start(s16[528,640]{1,0:T(8,128)(2,1)} %get-tuple-element.34), channel_id=1, source_target_pairs={{0,24},{8,0},{16,8},{24,16},{32,56},{40,32},{48,40},{56,48},{64,88... | collective-permute-start | bytes 2027528 | tf_op jit(solution)/shard_map/ppermute | solution.py:268
  139.5 59.3 %collective-permute-start.10 = (s16[528,640]{1,0:T(8,128)(2,1)}, s16[528,640]{1,0:T(8,128)(2,1)S(1)}, u32[]{:S(2)}, u32[]{:S(2)}) collective-permute-start(s16[528,640]{1,0:T(8,128)(2,1)} %get-tuple-element.42), channel_id=1, source_target_pairs={{0,8},{8,16},{16,24},{24,0},{32,40},{40,48},{48,56},{56,32},{64,72... | collective-permute-start | bytes 2027528 | tf_op jit(solution)/shard_map/ppermute | solution.py:268
  166.9 33.4 %collective-permute-start.9 = (s16[528,640]{1,0:T(8,128)(2,1)S(1)}, s16[528,640]{1,0:T(8,128)(2,1)S(1)}, u32[]{:S(2)}, u32[]{:S(2)}) collective-permute-start(s16[528,640]{1,0:T(8,128)(2,1)S(1)} %get-tuple-element.41), channel_id=1, source_target_pairs={{0,24},{8,0},{16,8},{24,16},{32,56},{40,32},{48,40},{56,48},{64,88... | collective-permute-start | bytes 2027528 | tf_op jit(solution)/shard_map/ppermute | solution.py:268
  170.9 29.4 %collective-permute-start.11 = (s16[528,640]{1,0:T(8,128)(2,1)}, s16[528,640]{1,0:T(8,128)(2,1)S(1)}, u32[]{:S(2)}, u32[]{:S(2)}) collective-permute-start(s16[528,640]{1,0:T(8,128)(2,1)} %get-tuple-element.43), channel_id=1, source_target_pairs={{0,24},{8,0},{16,8},{24,16},{32,56},{40,32},{48,40},{56,48},{64,88... | collective-permute-start | bytes 2027528 | tf_op jit(solution)/shard_map/ppermute | solution.py:268
  170.9 31.2 %collective-permute-start.8 = (s16[528,640]{1,0:T(8,128)(2,1)}, s16[528,640]{1,0:T(8,128)(2,1)S(1)}, u32[]{:S(2)}, u32[]{:S(2)}) collective-permute-start(s16[528,640]{1,0:T(8,128)(2,1)} %get-tuple-element.40), channel_id=1, source_target_pairs={{0,8},{8,16},{16,24},{24,0},{32,40},{40,48},{48,56},{56,32},{64,72... | collective-permute-start | bytes 2027528 | tf_op jit(solution)/shard_map/ppermute | solution.py:268
  176.7 1.9 copy-start.10
  198.7 15.6 %collective-permute-start.5 = (s16[528,640]{1,0:T(8,128)(2,1)S(1)}, s16[528,640]{1,0:T(8,128)(2,1)S(1)}, u32[]{:S(2)}, u32[]{:S(2)}) collective-permute-start(s16[528,640]{1,0:T(8,128)(2,1)S(1)} %get-tuple-element.36), channel_id=1, source_target_pairs={{0,96},{8,104},{16,112},{24,120},{32,0},{40,8},{48,16},{56,24},{64... | collective-permute-start | bytes 2027528 | tf_op jit(solution)/shard_map/ppermute | solution.py:268
  198.8 17.3 %collective-permute-start.6 = (s16[528,640]{1,0:T(8,128)(2,1)S(1)}, s16[528,640]{1,0:T(8,128)(2,1)S(1)}, u32[]{:S(2)}, u32[]{:S(2)}) collective-permute-start(s16[528,640]{1,0:T(8,128)(2,1)S(1)} %get-tuple-element.37), channel_id=1, source_target_pairs={{0,32},{8,40},{16,48},{24,56},{32,64},{40,72},{48,80},{56,88},{64,... | collective-permute-start | bytes 2027528 | tf_op jit(solution)/shard_map/ppermute | solution.py:268
  200.3 37.8 %collective-permute-start.4 = (s16[528,640]{1,0:T(8,128)(2,1)}, s16[528,640]{1,0:T(8,128)(2,1)S(1)}, u32[]{:S(2)}, u32[]{:S(2)}) collective-permute-start(s16[528,640]{1,0:T(8,128)(2,1)} %get-tuple-element.35), channel_id=1, source_target_pairs={{0,32},{8,40},{16,48},{24,56},{32,64},{40,72},{48,80},{56,88},{64,... | collective-permute-start | bytes 2027528 | tf_op jit(solution)/shard_map/ppermute | solution.py:268
  200.3 37.7 %collective-permute-start.7 = (s16[528,640]{1,0:T(8,128)(2,1)}, s16[528,640]{1,0:T(8,128)(2,1)S(1)}, u32[]{:S(2)}, u32[]{:S(2)}) collective-permute-start(s16[528,640]{1,0:T(8,128)(2,1)} %get-tuple-element.38), channel_id=1, source_target_pairs={{0,96},{8,104},{16,112},{24,120},{32,0},{40,8},{48,16},{56,24},{64... | collective-permute-start | bytes 2027528 | tf_op jit(solution)/shard_map/ppermute | solution.py:268
  204.9 37.4 %collective-permute-start.15 = (s16[272,640]{1,0:T(8,128)(2,1)S(1)}, s16[272,640]{1,0:T(8,128)(2,1)S(1)}, u32[]{:S(2)}, u32[]{:S(2)}) collective-permute-start(s16[272,640]{1,0:T(8,128)(2,1)S(1)} %get-tuple-element.48), channel_id=1, source_target_pairs={{0,32},{8,40},{16,48},{24,56},{32,64},{40,72},{48,80},{56,88},{64,... | collective-permute-start | bytes 1044488 | tf_op jit(solution)/shard_map/ppermute | solution.py:268
  214.3 32.5 %collective-permute-start.16 = (s16[272,640]{1,0:T(8,128)(2,1)}, s16[272,640]{1,0:T(8,128)(2,1)}, u32[]{:S(2)}, u32[]{:S(2)}) collective-permute-start(s16[272,640]{1,0:T(8,128)(2,1)} %get-tuple-element.49), channel_id=1, source_target_pairs={{0,64},{8,72},{16,80},{24,88},{32,96},{40,104},{48,112},{56,120},{... | collective-permute-start | bytes 1044488 | tf_op jit(solution)/shard_map/ppermute | solution.py:268
  216.1 30.8 %collective-permute-start.17 = (s16[272,640]{1,0:T(8,128)(2,1)}, s16[272,640]{1,0:T(8,128)(2,1)}, u32[]{:S(2)}, u32[]{:S(2)}) collective-permute-start(s16[272,640]{1,0:T(8,128)(2,1)} %get-tuple-element.50), channel_id=1, source_target_pairs={{0,96},{8,104},{16,112},{24,120},{32,0},{40,8},{48,16},{56,24},{64... | collective-permute-start | bytes 1044488 | tf_op jit(solution)/shard_map/ppermute | solution.py:268
  240.6 0.8 copy-start.2
  241.4 17.7 %collective-permute-start.12 = (s16[272,640]{1,0:T(8,128)(2,1)}, s16[272,640]{1,0:T(8,128)(2,1)}, u32[]{:S(2)}, u32[]{:S(2)}) collective-permute-start(s16[272,640]{1,0:T(8,128)(2,1)} %get-tuple-element.45), channel_id=1, source_target_pairs={{0,8},{8,16},{16,24},{24,0},{32,40},{40,48},{48,56},{56,32},{64,72... | collective-permute-start | bytes 1044488 | tf_op jit(solution)/shard_map/ppermute | solution.py:268
  241.4 17.7 %collective-permute-start.13 = (s16[272,640]{1,0:T(8,128)(2,1)}, s16[272,640]{1,0:T(8,128)(2,1)}, u32[]{:S(2)}, u32[]{:S(2)}) collective-permute-start(s16[272,640]{1,0:T(8,128)(2,1)} %get-tuple-element.46), channel_id=1, source_target_pairs={{0,16},{8,24},{16,0},{24,8},{32,48},{40,56},{48,32},{56,40},{64,80... | collective-permute-start | bytes 1044488 | tf_op jit(solution)/shard_map/ppermute | solution.py:268
  242.3 0.8 copy-start.4
  243.0 17.0 %collective-permute-start.14 = (s16[272,640]{1,0:T(8,128)(2,1)}, s16[272,640]{1,0:T(8,128)(2,1)}, u32[]{:S(2)}, u32[]{:S(2)}) collective-permute-start(s16[272,640]{1,0:T(8,128)(2,1)} %get-tuple-element.47), channel_id=1, source_target_pairs={{0,24},{8,0},{16,8},{24,16},{32,56},{40,32},{48,40},{56,48},{64,88... | collective-permute-start | bytes 1044488 | tf_op jit(solution)/shard_map/ppermute | solution.py:268
  244.9 15.2 %copy-start.3 = (f32[256,640]{1,0:T(8,128)S(1)}, f32[256,640]{1,0:T(8,128)}, u32[]{:S(2)}) copy-start(f32[256,640]{1,0:T(8,128)} %copy-done.2) | copy-start | bytes 1966084
  244.9 15.2 %copy-start.5 = (s16[272,640]{1,0:T(8,128)(2,1)S(1)}, s16[272,640]{1,0:T(8,128)(2,1)}, u32[]{:S(2)}) copy-start(s16[272,640]{1,0:T(8,128)(2,1)} %copy-done.4) | copy-start | bytes 1044484
Sparse Core Ops, SparseCore 0:
  10.3 71.6 all-gather.3
